TPU v7x, 32 devices: a whole 2x2x4 slice. The times are simulated.
32 devices in a mesh: px: 4 (over x, core), py: 8 (over z, y).
Axes of the slice: x: 2, y: 2, z: 4, core: 2. Of those that a mesh axis runs over, the one named last changes fastest.
Arguments:
- centroids: float32 [3, 524288], P(None, ('px', 'py')), may hold values from 0 to 3
- volumes: float32 [524288], P(('px', 'py')), may hold values from 0.3 to 3
- densities: float32 [524288], P(('px', 'py')), may hold values from 0.01 to 1
- sens_in: float32 [524288], P(('px', 'py')), may hold values from -192 to 192
- local_first: int32 [2048], P(('px', 'py')), may hold values from 0 to 62, as said below
- local_second: int32 [2048], P(('px', 'py')), may hold values from 1 to 63, as said below
- pair_count: int32 [32, 32], P(('px', 'py')), may hold values from 0 to 4, as said below
- pair_mine: int32 [32, 32, 4], P(('px', 'py')), may hold values from 0 to 63, as said below
Outputs:
- filtered: float32 [524288], P(('px', 'py'))
- sensitivity: float32 [524288], P(('px', 'py'))
Inputs may be any that keep to these rules, and one draw needn't show every extreme that they name: `pair_count`: Symmetric, zero on the diagonal, 1 to 4 elsewhere; some partition has 4 pairs with every other one. `pair_mine`: the 4 entries for one d and p are distinct; slot s of (d, p) and slot s of (p, d) name the same pair; slots at or past pair_count[d, p] are unused. local_first < local_second; no pair repeats within a partition. `local_second`: as for local_first.
All inputs are finite; a program needn't handle non-finite values.
Results may differ from a plain program's by a relative error of at most 0.004.
Values may be sent and summed in bfloat16 or wider, within the bound.
No kernel may reach another device: no remote copies, remote signals or barrier semaphores. Data moves between devices by JAX's collectives and lax.ppermute only.
A program may use at most 64 MiB of HBM per device.

v0:
```python
import math

import jax
import jax.numpy as jnp
from jax import lax
from jax.sharding import PartitionSpec as P

BLK = 256


radius = 1.0


def tile_weights(first, second):
    gap_x = first[..., 0, :, None] - second[..., 0, None, :]
    gap_y = first[..., 1, :, None] - second[..., 1, None, :]
    gap_z = first[..., 2, :, None] - second[..., 2, None, :]
    spread = jnp.sqrt(gap_x * gap_x + gap_y * gap_y + gap_z * gap_z)
    return jnp.maximum(radius - spread, 0.0).astype(jnp.bfloat16)


def pair_terms(weights, near_u, far_u):
    to_near = jnp.einsum("...ij,...cj->...ci", weights, far_u, preferred_element_type=jnp.float32)
    to_far = jnp.einsum("...ij,...ci->...cj", weights, near_u, preferred_element_type=jnp.float32)
    return (to_near, to_far)


def local_plan(blocks, first, second):
    own = jnp.arange(blocks, dtype=jnp.int32)
    near_ids = jnp.concatenate([own, first])
    far_ids = jnp.concatenate([own, second])
    twoway = jnp.concatenate(
        [jnp.zeros((blocks,), jnp.float32), jnp.ones((first.shape[0],), jnp.float32)]
    )
    count = near_ids.shape[0]
    group = math.gcd(count, 16)
    turns = count // group
    return (
        near_ids.reshape(turns, group),
        far_ids.reshape(turns, group),
        twoway.reshape(turns, group),
    )


def local_totals(cent, values, plan, kept):
    blocks = cent.shape[0]
    labels = jnp.arange(blocks, dtype=jnp.int32)

    def local_step(total, item):
        near, far, both, stored = item
        weights = tile_weights(cent[near], cent[far])
        to_near, to_far = pair_terms(weights, values[near], values[far])
        near_hot = (near[:, None] == labels[None, :]).astype(jnp.float32)
        far_hot = (far[:, None] == labels[None, :]).astype(jnp.float32) * both[:, None]
        total = total + jnp.einsum(
            "gb,gck->bck", near_hot, to_near, precision=lax.Precision.HIGHEST
        )
        total = total + jnp.einsum("gb,gck->bck", far_hot, to_far, precision=lax.Precision.HIGHEST)
        return (total, None)

    start = jnp.zeros(values.shape, jnp.float32)
    total, tiles = lax.scan(local_step, start, plan + (kept,))
    return (total, tiles)


def cross_totals(cent, values, far_cent, far_values, near_ids, mask, kept):
    blocks = cent.shape[0]
    peers, slots = near_ids.shape
    group = math.gcd(peers, 8)
    turns = peers // group
    labels = jnp.arange(blocks, dtype=jnp.int32)
    width = values.shape[1]
    cells = values.shape[2]

    def cross_step(total, item):
        near, live, other_cent, other_values, stored = item
        weights = tile_weights(cent[near], other_cent)
        to_near, to_far = pair_terms(weights, values[near], other_values)
        hot = (near[:, :, None] == labels[None, None, :]).astype(jnp.float32) * live[:, :, None]
        total = total + jnp.einsum("gkb,gkcx->bcx", hot, to_near, precision=lax.Precision.HIGHEST)
        far_part = to_far * live[:, :, None, None]
        tile_part = None
        return (total, (far_part, tile_part))

    cent_items = far_cent.reshape((turns, group, slots) + far_cent.shape[2:])
    start = jnp.zeros(values.shape, jnp.float32)
    items = (
        near_ids.reshape(turns, group, slots),
        mask.reshape(turns, group, slots),
        cent_items,
        far_values.reshape((turns, group, slots) + far_values.shape[2:]),
        kept,
    )
    total, outputs = lax.scan(cross_step, start, items)
    far_terms, tiles = outputs
    far_terms = far_terms.reshape(peers, slots, width, cells)
    return (total, far_terms, tiles)


def shards(
    centroids, volumes, densities, sens_in, local_first, local_second, pair_count, pair_mine
):
    blocks = volumes.shape[0] // BLK
    cent = centroids.reshape(3, blocks, BLK).transpose(1, 0, 2)
    weighted = jnp.stack([volumes, volumes * densities]).astype(jnp.bfloat16)
    weighted = weighted.reshape(2, blocks, BLK).transpose(1, 0, 2)
    counts = pair_count[0]
    chosen = pair_mine[0]
    peers = lax.axis_size(("px", "py"))
    slots = chosen.shape[1]
    me = lax.axis_index(("px", "py"))
    peer_ids = jnp.arange(peers, dtype=jnp.int32)
    labels = jnp.arange(blocks, dtype=jnp.int32)
    live = jnp.arange(slots, dtype=jnp.int32)[None, :] < counts[:, None]
    payload = jnp.concatenate([cent, weighted.astype(jnp.float32)], axis=1)
    received = lax.all_to_all(
        payload[chosen], ("px", "py"), split_axis=0, concat_axis=0, tiled=True
    )
    mask = (live & (me < peer_ids)[:, None]).astype(jnp.float32)
    back_hot = (chosen[:, :, None] == labels[None, None, :]).astype(jnp.float32)
    far_cent = received[:, :, :3]
    far_values = received[:, :, 3:].astype(jnp.bfloat16)
    plan = local_plan(blocks, local_first, local_second)
    totals, local_tiles = local_totals(cent, weighted, plan, None)
    cross_sum, far_terms, cross_tiles = cross_totals(
        cent, weighted, far_cent, far_values, chosen, mask, None
    )
    totals = totals + cross_sum
    returned = lax.all_to_all(far_terms, ("px", "py"), split_axis=0, concat_axis=0, tiled=True)
    totals = totals + jnp.einsum(
        "pkb,pkcx->bcx", back_hot, returned, precision=lax.Precision.HIGHEST
    )
    filtered = (totals[:, 1] / totals[:, 0]).reshape(-1)
    ratio = (sens_in.reshape(blocks, BLK) / totals[:, 0]).astype(jnp.bfloat16)[:, None, :]
    far_ratio = lax.all_to_all(ratio[chosen], ("px", "py"), split_axis=0, concat_axis=0, tiled=True)
    adjoint, unused_local = local_totals(cent, ratio, plan, local_tiles)
    cross_back, far_back, unused_cross = cross_totals(
        cent, ratio, far_cent, far_ratio, chosen, mask, cross_tiles
    )
    adjoint = adjoint + cross_back
    returned_back = lax.all_to_all(far_back, ("px", "py"), split_axis=0, concat_axis=0, tiled=True)
    adjoint = adjoint + jnp.einsum(
        "pkb,pkcx->bcx", back_hot, returned_back, precision=lax.Precision.HIGHEST
    )
    sensitivity = volumes * adjoint[:, 0].reshape(-1)
    return (filtered, sensitivity)


def solution(mesh):
    return jax.shard_map(
        shards,
        mesh=mesh,
        in_specs=(
            P(None, ("px", "py")),
            P(("px", "py")),
            P(("px", "py")),
            P(("px", "py")),
            P(("px", "py")),
            P(("px", "py")),
            P(("px", "py"), None),
            P(("px", "py"), None, None),
        ),
        out_specs=(P(("px", "py")), P(("px", "py"))),
        check_vma=False,
    )
```

profile of v0, /device:TPU:0, one launch (start us, length us, event | category | flops | bytes accessed | tf_op | source)
XLA Modules:
  0.0 340.7 jit_solution(2271094950656824469)
XLA Ops:
  4.7 7.3 %all-to-all-start = ((f32[32,4,5,256]{3,1,2,0:T(4,128)}), f32[32,4,5,256]{3,1,2,0:T(4,128)S(1)}, u32[]{:S(2)}, u32[]{:S(2)}) async-start(f32[32,4,5,256]{3,1,2,0:T(4,128)} %copy.68), calls=%async_computation | async-start | bytes 1310720 | tf_op jit(solution)/shard_map/all_to_all | solution.py:116
  13.7 17.5 %all-to-all-done = f32[32,4,5,256]{3,1,2,0:T(4,128)S(1)} async-done(((f32[32,4,5,256]{3,1,2,0:T(4,128)}), f32[32,4,5,256]{3,1,2,0:T(4,128)S(1)}, u32[]{:S(2)}, u32[]{:S(2)}) %all-to-all-start) | async-done | bytes 655392 | tf_op jit(solution)/shard_map/all_to_all | solution.py:116
  31.3 61.3 %while.50 = (s32[]{:T(128)}, f32[64,2,256]{2,0,1:T(8,128)S(1)}, f32[4,8,4,2,256]{4,2,3,1,0:T(4,128)}, s32[4,8,4]{1,2,0:T(4,128)S(1)}, f32[4,8,4]{1,2,0:T(4,128)S...) while((s32[]{:T(128)}, f32[64,2,256]{2,0,1:T(8,128)S(1)}, ...), condition=%wide.region_3.4_spmd.clone, body=%wide.region_2.3_spmd.clone.sunk | while | flops 75584608 | bytes 2169739 | solution.py:94
  33.0 6.2 %fusion.164 = f32[1,8,4,2,256]{4,3,2,1,0:T(2,128)S(1)} fusion(bf16[8,4,2,256]{3,2,1,0:T(2,128)(2,1)S(1)} %bitcast.354, f32[8,4,256]{2,1,0:T(4,128)S(1)} %get-tuple-element.741, f32[8,4,256]{2,1,0:T(4,128)S(1)} %get-tuple-element.744, f32[8,4,256]{2,1,0:T(4,128)S(1)} %get-tuple-element.745, f32[8,4,256]{2,1,0:T(4,128)S(1)} %get-tuple-element.746, ...), kind=kOutput, calls=%fused_computation.24.clone.1 | convolution fusion | flops 31473664 | bytes 295040 | tf_op jit(solution)/shard_map/while/body/eval_jaxpr/...ij,...ci->...cj/dot_general | solution.py:24
  39.9 6.3 %fusion.162 = f32[8,4,2,256]{3,2,1,0:T(2,128)S(1)} fusion(f32[8,4,256]{2,1,0:T(4,128)S(1)} %get-tuple-element.741, f32[8,4,256]{2,1,0:T(4,128)S(1)} %get-tuple-element.744, f32[8,4,256]{2,1,0:T(4,128)S(1)} %get-tuple-element.745, f32[8,4,256]{2,1,0:T(4,128)S(1)} %get-tuple-element.746, f32[8,4,256]{2,1,0:T(4,128)S(1)} %get-tuple-element.747, ...), kind=kOutput, calls=%fused_computation.20.clone.1 | convolution fusion | flops 31457280 | bytes 294912 | tf_op jit(solution)/shard_map/while/body/eval_jaxpr/...ij,...cj->...ci/dot_general | solution.py:23
  48.3 6.2 %fusion.164 = f32[1,8,4,2,256]{4,3,2,1,0:T(2,128)S(1)} fusion(bf16[8,4,2,256]{3,2,1,0:T(2,128)(2,1)S(1)} %bitcast.354, f32[8,4,256]{2,1,0:T(4,128)S(1)} %get-tuple-element.741, f32[8,4,256]{2,1,0:T(4,128)S(1)} %get-tuple-element.744, f32[8,4,256]{2,1,0:T(4,128)S(1)} %get-tuple-element.745, f32[8,4,256]{2,1,0:T(4,128)S(1)} %get-tuple-element.746, ...), kind=kOutput, calls=%fused_computation.24.clone.1 | convolution fusion | flops 31473664 | bytes 295040 | tf_op jit(solution)/shard_map/while/body/eval_jaxpr/...ij,...ci->...cj/dot_general | solution.py:24
  55.2 6.3 %fusion.162 = f32[8,4,2,256]{3,2,1,0:T(2,128)S(1)} fusion(f32[8,4,256]{2,1,0:T(4,128)S(1)} %get-tuple-element.741, f32[8,4,256]{2,1,0:T(4,128)S(1)} %get-tuple-element.744, f32[8,4,256]{2,1,0:T(4,128)S(1)} %get-tuple-element.745, f32[8,4,256]{2,1,0:T(4,128)S(1)} %get-tuple-element.746, f32[8,4,256]{2,1,0:T(4,128)S(1)} %get-tuple-element.747, ...), kind=kOutput, calls=%fused_computation.20.clone.1 | convolution fusion | flops 31457280 | bytes 294912 | tf_op jit(solution)/shard_map/while/body/eval_jaxpr/...ij,...cj->...ci/dot_general | solution.py:23
  63.6 6.2 %fusion.164 = f32[1,8,4,2,256]{4,3,2,1,0:T(2,128)S(1)} fusion(bf16[8,4,2,256]{3,2,1,0:T(2,128)(2,1)S(1)} %bitcast.354, f32[8,4,256]{2,1,0:T(4,128)S(1)} %get-tuple-element.741, f32[8,4,256]{2,1,0:T(4,128)S(1)} %get-tuple-element.744, f32[8,4,256]{2,1,0:T(4,128)S(1)} %get-tuple-element.745, f32[8,4,256]{2,1,0:T(4,128)S(1)} %get-tuple-element.746, ...), kind=kOutput, calls=%fused_computation.24.clone.1 | convolution fusion | flops 31473664 | bytes 295040 | tf_op jit(solution)/shard_map/while/body/eval_jaxpr/...ij,...ci->...cj/dot_general | solution.py:24
  70.5 6.3 %fusion.162 = f32[8,4,2,256]{3,2,1,0:T(2,128)S(1)} fusion(f32[8,4,256]{2,1,0:T(4,128)S(1)} %get-tuple-element.741, f32[8,4,256]{2,1,0:T(4,128)S(1)} %get-tuple-element.744, f32[8,4,256]{2,1,0:T(4,128)S(1)} %get-tuple-element.745, f32[8,4,256]{2,1,0:T(4,128)S(1)} %get-tuple-element.746, f32[8,4,256]{2,1,0:T(4,128)S(1)} %get-tuple-element.747, ...), kind=kOutput, calls=%fused_computation.20.clone.1 | convolution fusion | flops 31457280 | bytes 294912 | tf_op jit(solution)/shard_map/while/body/eval_jaxpr/...ij,...cj->...ci/dot_general | solution.py:23
  78.9 6.2 %fusion.164 = f32[1,8,4,2,256]{4,3,2,1,0:T(2,128)S(1)} fusion(bf16[8,4,2,256]{3,2,1,0:T(2,128)(2,1)S(1)} %bitcast.354, f32[8,4,256]{2,1,0:T(4,128)S(1)} %get-tuple-element.741, f32[8,4,256]{2,1,0:T(4,128)S(1)} %get-tuple-element.744, f32[8,4,256]{2,1,0:T(4,128)S(1)} %get-tuple-element.745, f32[8,4,256]{2,1,0:T(4,128)S(1)} %get-tuple-element.746, ...), kind=kOutput, calls=%fused_computation.24.clone.1 | convolution fusion | flops 31473664 | bytes 295040 | tf_op jit(solution)/shard_map/while/body/eval_jaxpr/...ij,...ci->...cj/dot_general | solution.py:24
  85.9 6.3 %fusion.162 = f32[8,4,2,256]{3,2,1,0:T(2,128)S(1)} fusion(f32[8,4,256]{2,1,0:T(4,128)S(1)} %get-tuple-element.741, f32[8,4,256]{2,1,0:T(4,128)S(1)} %get-tuple-element.744, f32[8,4,256]{2,1,0:T(4,128)S(1)} %get-tuple-element.745, f32[8,4,256]{2,1,0:T(4,128)S(1)} %get-tuple-element.746, f32[8,4,256]{2,1,0:T(4,128)S(1)} %get-tuple-element.747, ...), kind=kOutput, calls=%fused_computation.20.clone.1 | convolution fusion | flops 31457280 | bytes 294912 | tf_op jit(solution)/shard_map/while/body/eval_jaxpr/...ij,...cj->...ci/dot_general | solution.py:23
  95.2 82.5 %while.52 = (s32[]{:T(128)}, f32[64,2,256]{2,0,1:T(8,128)S(1)}, s32[8,16]{1,0:T(8,128)S(1)}, s32[8,16]{1,0:T(8,128)S(1)}, bf16[64,2,256]{2,1,0:T(2,128)(2,1)S(1)...) while((s32[]{:T(128)}, f32[64,2,256]{2,0,1:T(8,128)S(1)}, ...), condition=%wide.region_1.2_spmd.clone.clone, body=%wide.region_0.1_spmd.clone.clone.sunk | while | flops 44143712 | bytes 1549619 | solution.py:62
  179.6 5.8 %all-to-all-start.2 = ((bf16[32,4,1,256]{3,1,2,0:T(4,128)(2,1)}), bf16[32,4,1,256]{3,1,2,0:T(4,128)(2,1)S(1)}, u32[]{:S(2)}, u32[]{:S(2)}) async-start(bf16[32,4,1,256]{3,1,2,0:T(4,128)(2,1)} %bitcast.14), calls=%async_computation.2 | async-start | bytes 131072 | tf_op jit(solution)/shard_map/all_to_all | solution.py:135
  185.5 7.2 %all-to-all-done.2 = bf16[32,4,1,256]{3,1,2,0:T(4,128)(2,1)S(1)} async-done(((bf16[32,4,1,256]{3,1,2,0:T(4,128)(2,1)}), bf16[32,4,1,256]{3,1,2,0:T(4,128)(2,1)S(1)}, u32[]{:S(2)}, u32[]{:S(2)}) %all-to-all-start.2) | async-done | bytes 65568 | tf_op jit(solution)/shard_map/all_to_all | solution.py:135
  192.7 61.9 %while.51 = (s32[]{:T(128)}, f32[64,1,256]{2,0,1:T(8,128)S(1)}, f32[4,8,4,1,256]{4,2,3,1,0:T(4,128)}, s32[4,8,4]{1,2,0:T(4,128)S(1)}, f32[4,8,4]{1,2,0:T(4,128)S...) while((s32[]{:T(128)}, f32[64,1,256]{2,0,1:T(8,128)S(1)}, ...), condition=%wide.region_7.8_spmd.clone, body=%wide.region_6.7_spmd.clone.sunk | while | flops 60863584 | bytes 2235275 | solution.py:94
  194.5 6.3 %fusion.173 = f32[8,4,1,256]{3,2,1,0:T(1,128)S(1)} fusion(bf16[8,4,256,1]{2,3,1,0:T(2,128)(2,1)S(1)} %reshape.577, f32[8,4,256]{2,1,0:T(4,128)S(1)} %get-tuple-element.760, f32[8,4,256]{2,1,0:T(4,128)S(1)} %get-tuple-element.763, f32[8,4,256]{2,1,0:T(4,128)S(1)} %get-tuple-element.764, f32[8,4,256]{2,1,0:T(4,128)S(1)} %get-tuple-element.765, ...), kind=kOutput, calls=%fused_computation.53.clone.1 | convolution fusion | flops 27262976 | bytes 245760 | tf_op jit(solution)/shard_map/while/body/eval_jaxpr/...ij,...ci->...cj/dot_general | solution.py:24
  201.5 6.3 %fusion.171 = f32[8,4,1,256]{3,2,1,0:T(1,128)S(1)} fusion(f32[8,4,256]{2,1,0:T(4,128)S(1)} %get-tuple-element.760, f32[8,4,256]{2,1,0:T(4,128)S(1)} %get-tuple-element.763, f32[8,4,256]{2,1,0:T(4,128)S(1)} %get-tuple-element.764, f32[8,4,256]{2,1,0:T(4,128)S(1)} %get-tuple-element.765, f32[8,4,256]{2,1,0:T(4,128)S(1)} %get-tuple-element.768, ...), kind=kOutput, calls=%fused_computation.54.clone.1 | convolution fusion | flops 27262976 | bytes 245760 | tf_op jit(solution)/shard_map/while/body/eval_jaxpr/...ij,...cj->...ci/dot_general | solution.py:23
  210.0 6.3 %fusion.173 = f32[8,4,1,256]{3,2,1,0:T(1,128)S(1)} fusion(bf16[8,4,256,1]{2,3,1,0:T(2,128)(2,1)S(1)} %reshape.577, f32[8,4,256]{2,1,0:T(4,128)S(1)} %get-tuple-element.760, f32[8,4,256]{2,1,0:T(4,128)S(1)} %get-tuple-element.763, f32[8,4,256]{2,1,0:T(4,128)S(1)} %get-tuple-element.764, f32[8,4,256]{2,1,0:T(4,128)S(1)} %get-tuple-element.765, ...), kind=kOutput, calls=%fused_computation.53.clone.1 | convolution fusion | flops 27262976 | bytes 245760 | tf_op jit(solution)/shard_map/while/body/eval_jaxpr/...ij,...ci->...cj/dot_general | solution.py:24
  217.0 6.3 %fusion.171 = f32[8,4,1,256]{3,2,1,0:T(1,128)S(1)} fusion(f32[8,4,256]{2,1,0:T(4,128)S(1)} %get-tuple-element.760, f32[8,4,256]{2,1,0:T(4,128)S(1)} %get-tuple-element.763, f32[8,4,256]{2,1,0:T(4,128)S(1)} %get-tuple-element.764, f32[8,4,256]{2,1,0:T(4,128)S(1)} %get-tuple-element.765, f32[8,4,256]{2,1,0:T(4,128)S(1)} %get-tuple-element.768, ...), kind=kOutput, calls=%fused_computation.54.clone.1 | convolution fusion | flops 27262976 | bytes 245760 | tf_op jit(solution)/shard_map/while/body/eval_jaxpr/...ij,...cj->...ci/dot_general | solution.py:23
  225.4 6.3 %fusion.173 = f32[8,4,1,256]{3,2,1,0:T(1,128)S(1)} fusion(bf16[8,4,256,1]{2,3,1,0:T(2,128)(2,1)S(1)} %reshape.577, f32[8,4,256]{2,1,0:T(4,128)S(1)} %get-tuple-element.760, f32[8,4,256]{2,1,0:T(4,128)S(1)} %get-tuple-element.763, f32[8,4,256]{2,1,0:T(4,128)S(1)} %get-tuple-element.764, f32[8,4,256]{2,1,0:T(4,128)S(1)} %get-tuple-element.765, ...), kind=kOutput, calls=%fused_computation.53.clone.1 | convolution fusion | flops 27262976 | bytes 245760 | tf_op jit(solution)/shard_map/while/body/eval_jaxpr/...ij,...ci->...cj/dot_general | solution.py:24
  232.5 6.3 %fusion.171 = f32[8,4,1,256]{3,2,1,0:T(1,128)S(1)} fusion(f32[8,4,256]{2,1,0:T(4,128)S(1)} %get-tuple-element.760, f32[8,4,256]{2,1,0:T(4,128)S(1)} %get-tuple-element.763, f32[8,4,256]{2,1,0:T(4,128)S(1)} %get-tuple-element.764, f32[8,4,256]{2,1,0:T(4,128)S(1)} %get-tuple-element.765, f32[8,4,256]{2,1,0:T(4,128)S(1)} %get-tuple-element.768, ...), kind=kOutput, calls=%fused_computation.54.clone.1 | convolution fusion | flops 27262976 | bytes 245760 | tf_op jit(solution)/shard_map/while/body/eval_jaxpr/...ij,...cj->...ci/dot_general | solution.py:23
  240.9 6.3 %fusion.173 = f32[8,4,1,256]{3,2,1,0:T(1,128)S(1)} fusion(bf16[8,4,256,1]{2,3,1,0:T(2,128)(2,1)S(1)} %reshape.577, f32[8,4,256]{2,1,0:T(4,128)S(1)} %get-tuple-element.760, f32[8,4,256]{2,1,0:T(4,128)S(1)} %get-tuple-element.763, f32[8,4,256]{2,1,0:T(4,128)S(1)} %get-tuple-element.764, f32[8,4,256]{2,1,0:T(4,128)S(1)} %get-tuple-element.765, ...), kind=kOutput, calls=%fused_computation.53.clone.1 | convolution fusion | flops 27262976 | bytes 245760 | tf_op jit(solution)/shard_map/while/body/eval_jaxpr/...ij,...ci->...cj/dot_general | solution.py:24
  248.0 6.3 %fusion.171 = f32[8,4,1,256]{3,2,1,0:T(1,128)S(1)} fusion(f32[8,4,256]{2,1,0:T(4,128)S(1)} %get-tuple-element.760, f32[8,4,256]{2,1,0:T(4,128)S(1)} %get-tuple-element.763, f32[8,4,256]{2,1,0:T(4,128)S(1)} %get-tuple-element.764, f32[8,4,256]{2,1,0:T(4,128)S(1)} %get-tuple-element.765, f32[8,4,256]{2,1,0:T(4,128)S(1)} %get-tuple-element.768, ...), kind=kOutput, calls=%fused_computation.54.clone.1 | convolution fusion | flops 27262976 | bytes 245760 | tf_op jit(solution)/shard_map/while/body/eval_jaxpr/...ij,...cj->...ci/dot_general | solution.py:23
  257.2 81.8 %while.53 = (s32[]{:T(128)}, f32[64,1,256]{2,0,1:T(8,128)S(1)}, s32[8,16]{1,0:T(8,128)S(1)}, s32[8,16]{1,0:T(8,128)S(1)}, bf16[64,1,256]{2,0,1:T(8,128)(2,1)S(1)...) while((s32[]{:T(128)}, f32[64,1,256]{2,0,1:T(8,128)S(1)}, ...), condition=%wide.region_5.6_spmd.clone.clone, body=%wide.region_4.5_spmd.clone.clone.sunk | while | flops 33608800 | bytes 1172787 | solution.py:62
  259.2 3.1 fusion.200
  269.4 3.1 fusion.200
  279.6 3.1 fusion.200
  289.9 3.1 fusion.200
  300.1 3.1 fusion.200
  310.3 3.1 fusion.200
  320.6 3.1 fusion.200
  330.8 3.1 fusion.200
  (539 shorter events, 173.7 us)
Async XLA Ops:
  0.6 2.1 copy-start
  4.7 7.3 %copy-start.3 = (s32[1,32,4]{1,2,0:T(4,128)S(1)}, s32[1,32,4]{1,2,0:T(4,128)}, u32[]{:S(2)}) copy-start(s32[1,32,4]{1,2,0:T(4,128)} %param.23) | copy-start | bytes 1540
  4.7 8.0 %copy-start.6 = (s32[1,32]{1,0:T(1,128)S(1)}, s32[1,32]{1,0:T(1,128)}, u32[]{:S(2)}) copy-start(s32[1,32]{1,0:T(1,128)} %param.22) | copy-start | bytes 388
  4.7 8.8 %copy-start.4 = (s32[64]{0:T(128)S(1)}, s32[64]{0:T(128)}, u32[]{:S(2)}) copy-start(s32[64]{0:T(128)} %param.20) | copy-start | bytes 772
  4.7 8.8 %copy-start.5 = (s32[64]{0:T(128)S(1)}, s32[64]{0:T(128)}, u32[]{:S(2)}) copy-start(s32[64]{0:T(128)} %param.21) | copy-start | bytes 772
  4.7 26.5 %all-to-all-start = ((f32[32,4,5,256]{3,1,2,0:T(4,128)}), f32[32,4,5,256]{3,1,2,0:T(4,128)S(1)}, u32[]{:S(2)}, u32[]{:S(2)}) async-start(f32[32,4,5,256]{3,1,2,0:T(4,128)} %copy.68), calls=%async_computation | async-start | bytes 1310720 | tf_op jit(solution)/shard_map/all_to_all | solution.py:116
  92.5 85.2 %all-to-all-start.1 = ((f32[32,4,2,256]{3,1,2,0:T(4,128)}), f32[32,4,2,256]{3,1,2,0:T(4,128)S(1)}, u32[]{:S(2)}, u32[]{:S(2)}) async-start(f32[32,4,2,256]{3,1,2,0:T(4,128)} %bitcast.10), calls=%async_computation.1 | async-start | bytes 524288 | tf_op jit(solution)/shard_map/all_to_all | solution.py:129
  95.1 82.5 %copy-start.2 = (f32[16384]{0:T(1024)S(1)}, f32[16384]{0:T(1024)}, u32[]{:S(2)}) copy-start(f32[16384]{0:T(1024)} %param.19) | copy-start | bytes 196612
  179.6 13.1 %all-to-all-start.2 = ((bf16[32,4,1,256]{3,1,2,0:T(4,128)(2,1)}), bf16[32,4,1,256]{3,1,2,0:T(4,128)(2,1)S(1)}, u32[]{:S(2)}, u32[]{:S(2)}) async-start(bf16[32,4,1,256]{3,1,2,0:T(4,128)(2,1)} %bitcast.14), calls=%async_computation.2 | async-start | bytes 131072 | tf_op jit(solution)/shard_map/all_to_all | solution.py:135
  254.6 85.1 %all-to-all-start.3 = ((f32[32,4,1,256]{3,1,2,0:T(4,128)}), f32[32,4,1,256]{3,1,2,0:T(4,128)S(1)}, u32[]{:S(2)}, u32[]{:S(2)}) async-start(f32[32,4,1,256]{3,1,2,0:T(4,128)} %bitcast.90), calls=%async_computation.3 | async-start | bytes 262144 | tf_op jit(solution)/shard_map/all_to_all | solution.py:141
  257.2 82.9 %copy-start.1 = (f32[16384]{0:T(1024)S(1)}, f32[16384]{0:T(1024)}, u32[]{:S(2)}) copy-start(f32[16384]{0:T(1024)} %param.17) | copy-start | bytes 196612
where the time goes:
time: 342 us; the launch traced here: 341 us
  matrix products  215 us (63%)
  local copies, waits for them, and re-layouts  72.5 us (21%)
  waiting for transfers between devices  24.7 us (7%)
  starting transfers between devices  18.3 us (5%)
  other arithmetic  6.38 us (2%)
    dot_general x24, matrix products, pair_terms(): jnp.einsum('...ij,...cj->...ci', weights, far_u, preferred_element_type=j...  100 us
    dot_general x24, matrix products, pair_terms(): jnp.einsum('...ij,...ci->...cj', weights, near_u, preferred_element_type=...  100 us
    gather x32, local copies, waits for them, and re-layouts, local_step(): to_near, to_far = pair_terms(weights, values[near], values[far])  19 us
    gather x32, local copies, waits for them, and re-layouts, local_step(): weights = tile_weights(cent[near], cent[far])  19 us
    all_to_all x1, waiting for transfers between devices, shards(): lax.all_to_all(payload[chosen], ('px', 'py'), split_axis=0, concat_axis=0...  17.5 us
    mul x16, local copies, waits for them, and re-layouts, local_step(): (far[:, None] == labels[None, :]).astype(jnp.float32) * both[:, None]  11.1 us
    all_to_all x1, starting transfers between devices, shards(): lax.all_to_all(payload[chosen], ('px', 'py'), split_axis=0, concat_axis=0...  7.3 us
    all_to_all x1, waiting for transfers between devices, shards(): lax.all_to_all(ratio[chosen], ('px', 'py'), split_axis=0, concat_axis=0,...  7.25 us
  transfers between devices with their start and end apart: 4, of which 2 were waited for; matrix products, arithmetic and copies ran while one was open for 48% of the time, Pallas kernels for 0%

commit v1 on v0

v1 whole, which is shorter than its diff:
```python
import functools

import jax
import jax.numpy as jnp
from jax import lax
from jax.experimental import pallas as pl
from jax.experimental.pallas import tpu as pltpu
from jax.sharding import PartitionSpec as P

BLK = 256
HALF = BLK // 2
AXES = ("px", "py")
ROWS = 8
WORDS = 5
PEER_ROWS = 24
FEATURES = 32
COORD = 16384.0
VOLUME = 21845.0
DENSITY = 65535.0
MIDDLE = 1.5
TINY = 1e-12
KEEP_LIMIT = 20 << 20
MIB = 1 << 20

VMEM = pl.BlockSpec(memory_space=pltpu.VMEM)
SMEM = pl.BlockSpec(memory_space=pltpu.SMEM)
HBM = pl.BlockSpec(memory_space=pltpu.HBM)


def fixed(value, steps):
    return (value * steps + 0.5).astype(jnp.int32)


def two_halves(first, second):
    return first | (second << 16)


def pack_kernel(chosen_in, cent_in, vol_in, dens_in, payload, words, chosen, cent, vol, dens, sems):
    blocks = words.shape[0]
    waits = fetch(
        [(cent_in, cent), (vol_in, vol), (dens_in, dens), (chosen_in, chosen)], sems
    )
    words[...] = jnp.zeros_like(words)
    for wait in waits:
        wait()
    for b in range(blocks):
        low = cent[:, b * BLK : b * BLK + HALF]
        high = cent[:, b * BLK + HALF : (b + 1) * BLK]
        words[b, 0:3, :] = two_halves(fixed(low, COORD), fixed(high, COORD))
    for row, source, steps in ((3, vol, VOLUME), (4, dens, DENSITY)):
        low = source[pl.ds(0, blocks, stride=2), :]
        high = source[pl.ds(1, blocks, stride=2), :]
        words[:, row, :] = two_halves(fixed(low, steps), fixed(high, steps))
    slots, peers = chosen.shape

    def send(p, carry):
        for s in range(slots):
            payload[p, WORDS * s : WORDS * (s + 1), :] = words[chosen[s, p], 0:WORDS, :]
        return carry

    lax.fori_loop(0, peers, send, 0, unroll=4)


def decode(word):
    row = lax.broadcasted_iota(jnp.int32, (ROWS, BLK), 0)
    step = jnp.where(
        row < 3,
        1.0 / COORD,
        jnp.where(row == 3, 1.0 / VOLUME, jnp.where(row == 4, 1.0 / DENSITY, 0.0)),
    )
    parts = jnp.concatenate([word & 0xFFFF, lax.shift_right_logical(word, 16)], axis=1)
    held = parts.astype(jnp.float32) * step
    volume = held[3:4, :]
    values = jnp.where(row == 4, held * volume, held).astype(jnp.bfloat16)
    place = jnp.where(row < 3, held - MIDDLE, 0.0)
    high = place.astype(jnp.bfloat16).astype(jnp.float32)
    low = place - high
    norm = jnp.sum(place * place, axis=0, keepdims=True)
    norm1 = norm.astype(jnp.bfloat16).astype(jnp.float32)
    rest = norm - norm1
    norm2 = rest.astype(jnp.bfloat16).astype(jnp.float32)
    norm3 = rest - norm2
    one = jnp.where(row == 6, 1.0, 0.0)
    far1 = high + jnp.where(
        row == 3, norm1, jnp.where(row == 4, norm2, jnp.where(row == 5, norm3, one))
    )
    far2 = low + jnp.where((row == 3) | (row == 4), 1.0, 0.0)
    far = jnp.concatenate([far1, far2], axis=0).astype(jnp.bfloat16)
    far = jnp.concatenate([far, far], axis=0)
    near1 = -2.0 * high + jnp.where(
        (row >= 3) & (row <= 5), 1.0, jnp.where(row == 6, norm1, 0.0)
    )
    near2 = -2.0 * high + jnp.where(row == 3, norm2, jnp.where(row == 4, norm3, 0.0))
    near34 = -2.0 * low
    near = jnp.concatenate([near1, near2, near34, near34], axis=0).astype(jnp.bfloat16)
    return far, near, values


def product(rows, tile):
    return jnp.dot(rows, tile, preferred_element_type=jnp.float32)


def product_t(rows, tile):
    return lax.dot_general(
        rows, tile, (((1,), (1,)), ((), ())), preferred_element_type=jnp.float32
    )


def cone(square):
    square = jnp.maximum(square, TINY)
    return jnp.maximum((1.0 - square * lax.rsqrt(square)).astype(jnp.bfloat16), 0)


def staged(groups, width, tiles, kept, sems, squares, square, use):
    def copy(k):
        part = pl.ds(2 * k * width, 2 * width)
        return pltpu.make_async_copy(tiles.at[part], kept.at[part], sems.at[k])

    def distances(g, slot):
        for u in range(width):
            squares[slot][u] = square(g * width + u)

    def cones(view, at, slot):
        for u in range(width):
            view[at + u] = cone(squares[slot][u])

    def sums(view, at, g):
        return [use(g * width + u, view[at + u]) for u in range(width)]

    def finish(ends):
        for end in ends:
            end()

    distances(0, 0)
    cones(tiles.at[pl.ds(0, width)], 0, 0)
    distances(1, 1)

    def turn(k, carry):
        g = 2 * k
        view = tiles.at[pl.ds((g - 2) * width, 3 * width)]
        ends = sums(view, 0, g - 2)
        cones(view, width, 1)
        distances(g, 0)
        finish(ends)
        if kept is not None:
            copy(k - 1).start()
        ends = sums(view, width, g - 1)
        cones(view, 2 * width, 0)
        distances(g + 1, 1)
        finish(ends)
        return carry

    lax.fori_loop(1, groups // 2, turn, 0)
    view = tiles.at[pl.ds((groups - 2) * width, 2 * width)]
    finish(sums(view, 0, groups - 2))
    cones(view, width, 1)
    if kept is not None:
        copy(groups // 2 - 1).start()
    finish(sums(view, width, groups - 1))

    def wait():
        def one(k, carry):
            copy(k).wait()
            return carry

        lax.fori_loop(0, groups // 2, one, 0)

    return wait


def chunked(size, width, tiles, squares, square, use):
    room = tiles.shape[0]

    def chunk(c, carry):
        base = c * room
        left = jnp.minimum(size - base, room)
        groups = even_groups(left, width)
        staged(
            groups,
            width,
            tiles,
            None,
            None,
            squares,
            lambda i: square(base + i),
            lambda i, tile: use(base + i, tile),
        )
        return carry

    lax.fori_loop(0, jnp.maximum((size + room - 1) // room, 1), chunk, 0)


def even_groups(size, width):
    return jnp.maximum((size + 2 * width - 1) // (2 * width), 1) * 2


def fetch(pairs, sems):
    copies = [pltpu.make_async_copy(a, b, sems.at[k]) for k, (a, b) in enumerate(pairs)]
    for copy in copies:
        copy.start()
    return [copy.wait for copy in copies]


def local_kernel(
    width, first_in, second_in, counts_in, words, total, kept, near, listed, size,
    first, second, counts, tiles, far_t, vals, square0, square1, sems, self_sems, pair_sems,
):
    blocks = words.shape[0]
    pairs = first.shape[0]
    peers = counts.shape[1]
    slots = listed.shape[0] // peers
    squares = (square0, square1)
    waits = fetch([(first_in, first), (second_in, second), (counts_in, counts)], sems)

    def prepare(b, carry):
        f, n, v = decode(words[b])
        far_t[b] = f.T
        near[b] = n
        vals[b] = v
        return carry

    lax.fori_loop(0, blocks, prepare, 0, unroll=4)
    for wait in waits:
        wait()

    def square_self(b):
        return product(far_t[b], near[b])

    def use_self(b, tile):
        sums = product(vals[b], tile)

        def end():
            total[b] = sums

        return end

    part = pl.ds(0, blocks)
    wait_self = staged(
        blocks // width, width, tiles.at[part], kept.at[part], self_sems, squares, square_self, use_self
    )

    def square_pair(j):
        return product(far_t[second[j]], near[first[j]])

    def use_pair(j, tile):
        a, b = first[j], second[j]
        to_first = product(vals[b], tile)
        to_second = product_t(vals[a], tile)

        def end():
            total[a] += to_first
            total[b] += to_second

        return end

    part = pl.ds(blocks, pairs)
    wait_pair = staged(
        pairs // width, width, tiles.at[part], kept.at[part], pair_sems, squares, square_pair, use_pair
    )

    def collect(p, found):
        for s in range(slots):
            listed[found] = p * slots + s
            found = found + (s < counts[0, p]).astype(jnp.int32)
        return found

    found = lax.fori_loop(0, peers, collect, 0)
    size[0] = found

    def blank(i, carry):
        listed[i] = 0
        return carry

    lax.fori_loop(found, listed.shape[0], blank, 0)
    wait_self()
    wait_pair()


def far_word(received, slots, place):
    peer, slot = place // slots, place % slots
    return received[pl.ds(peer * PEER_ROWS + slot * WORDS, ROWS), :]


def cross_kernel(
    width, keep, listed, size, chosen_in, received, near, total_in, sens_in, filtered, ratio, payload, *rest
):
    kept = None
    if keep:
        kept, *rest = rest
    tiles, total, flat, vals, sens, chosen, square0, square1, sems, *tile_sems = rest
    blocks = near.shape[0]
    waits = fetch([(chosen_in, chosen), (sens_in, sens)], sems)
    total[...] = total_in[...]
    slots, peers = chosen.shape
    ring = vals.shape[0]
    for wait in waits:
        wait()

    def mine(place):
        return chosen[place % slots, place // slots]

    def square(i):
        place = listed[i]
        f, unused, v = decode(far_word(received, slots, place))
        vals[lax.rem(i, ring)] = v
        return product(f.T, near[mine(place)])

    def use(i, tile):
        b = mine(listed[i])
        sums = product(vals[lax.rem(i, ring)], tile)
        sums = jnp.where(i < size[0], sums, 0.0)

        def end():
            total[b] += sums

        return end

    squares = (square0, square1)
    if keep:
        groups = even_groups(size[0], width)
        wait_tiles = staged(groups, width, tiles, kept, tile_sems[0], squares, square, use)
    else:
        chunked(size[0], width, tiles, squares, square, use)
    base = total[:, 3, :]
    filt = total[:, 4, :] / base
    for half in range(2):
        rows = pl.ds(half, blocks, stride=2)
        lanes = slice(half * HALF, (half + 1) * HALF)
        filtered[rows, :] = filt[:, lanes]
        part = sens[rows, :] / base[:, lanes]
        flat[rows, :] = part.astype(jnp.bfloat16).astype(jnp.float32)
    ratio[...] = jnp.zeros_like(ratio)
    for half in range(2):
        lanes = slice(half * HALF, (half + 1) * HALF)
        ratio[:, 0, lanes] = flat[pl.ds(half, blocks, stride=2), :]

    def send(p, carry):
        for s in range(slots):
            payload[p, 2 * s : 2 * s + 2, :] = flat[pl.ds(2 * chosen[s, p], 2), :]
        return carry

    lax.fori_loop(0, peers, send, 0, unroll=4)
    if keep:
        wait_tiles()


def load_groups(width, groups, kept, tiles, sems):
    def copy(k):
        part = pl.ds(k * width, width)
        return pltpu.make_async_copy(kept.at[part], tiles.at[part], sems.at[k])

    def one(k, carry):
        copy(k).start()
        return carry

    lax.fori_loop(0, groups, one, 0)
    return lambda k: copy(k).wait()


def back_local_kernel(
    width, first_in, second_in, ratio, kept, total, first, second, tiles, sems, tile_sems
):
    blocks = ratio.shape[0]
    pairs = first.shape[0]
    waits = fetch([(first_in, first), (second_in, second)], sems)
    ready = load_groups(width, (blocks + pairs) // width, kept, tiles, tile_sems)

    def rows(b):
        return ratio[b].astype(jnp.bfloat16)

    def own(k, carry):
        ready(k)
        sums = [product(rows(k * width + u), tiles[k * width + u]) for u in range(width)]
        for u in range(width):
            total[k * width + u] = sums[u]
        return carry

    lax.fori_loop(0, blocks // width, own, 0)
    for wait in waits:
        wait()

    def pair(k, carry):
        ready(blocks // width + k)
        ids = [(first[k * width + u], second[k * width + u]) for u in range(width)]
        sums = []
        for u, (a, b) in enumerate(ids):
            tile = tiles[blocks + k * width + u]
            sums.append((product(rows(b), tile), product_t(rows(a), tile)))
        for (a, b), (to_first, to_second) in zip(ids, sums):
            total[a] += to_first
            total[b] += to_second
        return carry

    lax.fori_loop(0, pairs // width, pair, 0)


def far_ratio(ratio, place):
    row0 = ratio[pl.ds(place * 2, 1), :]
    row1 = ratio[pl.ds(place * 2 + 1, 1), :]
    return jnp.concatenate([row0, row1], axis=1).astype(jnp.bfloat16)


def finish_back(blocks, vol, total, out):
    for half in range(2):
        rows = pl.ds(half, blocks, stride=2)
        lanes = slice(half * HALF, (half + 1) * HALF)
        out[rows, :] = vol[rows, :] * total[:, 0, lanes]


def back_cross_kernel(
    width, listed, size, chosen_in, ratio, kept, total_in, vol_in, out,
    total, chosen, vol, tiles, sems, tile_sems,
):
    blocks = total.shape[0]
    groups = (size[0] + width - 1) // width
    waits = fetch([(chosen_in, chosen), (vol_in, vol)], sems)
    ready = load_groups(width, groups, kept, tiles, tile_sems)
    total[...] = total_in[...]
    slots = chosen.shape[0]
    for wait in waits:
        wait()

    def turn(k, carry):
        ready(k)
        sums = []
        for u in range(width):
            i = k * width + u
            place = listed[i]
            part = product(far_ratio(ratio, place), tiles[i])
            part = jnp.where(i < size[0], part, 0.0)
            sums.append((chosen[place % slots, place // slots], part))
        for b, part in sums:
            total[b, 0:1, :] += part
        return carry

    lax.fori_loop(0, groups, turn, 0)
    finish_back(blocks, vol, total, out)


def back_again_kernel(
    width, listed, size, chosen_in, ratio, received, near, total_in, vol_in, out,
    total, chosen, vol, tiles, square0, square1, sems,
):
    blocks = total.shape[0]
    waits = fetch([(chosen_in, chosen), (vol_in, vol)], sems)
    total[...] = total_in[...]
    slots = chosen.shape[0]
    for wait in waits:
        wait()

    def mine(place):
        return chosen[place % slots, place // slots]

    def square(i):
        place = listed[i]
        f, unused, v = decode(far_word(received, slots, place))
        return product(f.T, near[mine(place)])

    def use(i, tile):
        part = jnp.where(i < size[0], product(far_ratio(ratio, listed[i]), tile), 0.0)

        def end():
            total[mine(listed[i]), 0:1, :] += part

        return end

    chunked(size[0], width, tiles, (square0, square1), square, use)
    finish_back(blocks, vol, total, out)


def in_hbm(array):
    return pltpu.with_memory_space_constraint(array, pltpu.HBM)


def params(mib):
    return pltpu.CompilerParams(vmem_limit_bytes=mib * MIB)


def shards(
    centroids, volumes, densities, sens_in, local_first, local_second, pair_count, pair_mine
):
    elements = volumes.shape[0]
    blocks = elements // BLK
    flat_rows = elements // HALF
    vol = in_hbm(volumes.reshape(flat_rows, HALF))
    dens = in_hbm(densities.reshape(flat_rows, HALF))
    sens = in_hbm(sens_in.reshape(flat_rows, HALF))
    local_first, local_second = in_hbm(local_first), in_hbm(local_second)
    chosen = in_hbm(pair_mine[0].T)
    slots, peers = chosen.shape
    places = peers * slots
    pairs = local_first.shape[0]
    f32, bf16, i32 = jnp.float32, jnp.bfloat16, jnp.int32
    shape = jax.ShapeDtypeStruct
    width = 2
    flat = pltpu.VMEM((flat_rows, HALF), f32)
    sums = pltpu.VMEM((blocks, ROWS, BLK), f32)
    square = pltpu.VMEM((width, BLK, BLK), f32)
    table = pltpu.SMEM(chosen.shape, i32)
    row = pltpu.SMEM((pairs,), i32)

    payload, words = pl.pallas_call(
        pack_kernel,
        out_shape=(shape((peers, PEER_ROWS, HALF), i32), shape((blocks, ROWS, HALF), i32)),
        in_specs=[HBM] * 4,
        out_specs=(VMEM, VMEM),
        scratch_shapes=[
            table,
            pltpu.VMEM(centroids.shape, f32),
            flat,
            flat,
            pltpu.SemaphoreType.DMA((4,)),
        ],
        compiler_params=params(8),
        name="pack",
    )(chosen, in_hbm(centroids), vol, dens)
    received = lax.all_to_all(payload, AXES, split_axis=0, concat_axis=0, tiled=True)
    total, tiles, near, listed, size = pl.pallas_call(
        functools.partial(local_kernel, width),
        out_shape=(
            shape((blocks, ROWS, BLK), f32),
            pltpu.HBM((blocks + pairs, BLK, BLK), bf16),
            shape((blocks, FEATURES, BLK), bf16),
            shape((places,), i32),
            shape((1,), i32),
        ),
        in_specs=[HBM, HBM, HBM, VMEM],
        out_specs=(VMEM, HBM, VMEM, SMEM, SMEM),
        scratch_shapes=[
            row,
            row,
            pltpu.SMEM(pair_count.shape, i32),
            pltpu.VMEM((blocks + pairs, BLK, BLK), bf16),
            pltpu.VMEM((blocks, BLK, FEATURES), bf16),
            pltpu.VMEM((blocks, ROWS, BLK), bf16),
            square,
            square,
            pltpu.SemaphoreType.DMA((3,)),
            pltpu.SemaphoreType.DMA((blocks // (2 * width),)),
            pltpu.SemaphoreType.DMA((pairs // (2 * width),)),
        ],
        compiler_params=params(48),
        cost_estimate=pl.CostEstimate(
            flops=(blocks + pairs) * BLK * BLK * 100, bytes_accessed=1 << 20, transcendentals=0
        ),
        name="local",
    )(local_first, local_second, in_hbm(pair_count), words)
    received = received.reshape(peers * PEER_ROWS, HALF)
    tile_bytes = BLK * BLK * 2
    keep = places * tile_bytes <= KEEP_LIMIT
    held = places if keep else KEEP_LIMIT // tile_bytes // (4 * width) * (4 * width)
    filtered, ratio, payload2, *cross_tiles = pl.pallas_call(
        functools.partial(cross_kernel, width, keep),
        out_shape=(
            shape((flat_rows, HALF), f32),
            shape((blocks, ROWS, BLK), f32),
            shape((peers, 2 * slots, HALF), f32),
        )
        + ((pltpu.HBM((places, BLK, BLK), bf16),) if keep else ()),
        in_specs=[SMEM, SMEM, HBM, VMEM, VMEM, VMEM, HBM],
        out_specs=(VMEM, VMEM, VMEM) + ((HBM,) if keep else ()),
        scratch_shapes=[
            pltpu.VMEM((held, BLK, BLK), bf16),
            sums,
            flat,
            pltpu.VMEM((8 * width, ROWS, BLK), bf16),
            flat,
            table,
            square,
            square,
            pltpu.SemaphoreType.DMA((2,)),
        ]
        + ([pltpu.SemaphoreType.DMA((places // (2 * width),))] if keep else []),
        compiler_params=params(48),
        name="cross",
    )(listed, size, chosen, received, near, total, sens)
    received2 = lax.all_to_all(payload2, AXES, split_axis=0, concat_axis=0, tiled=True)
    back = pl.pallas_call(
        functools.partial(back_local_kernel, 8),
        out_shape=shape((blocks, ROWS, BLK), f32),
        in_specs=[HBM, HBM, VMEM, HBM],
        out_specs=VMEM,
        scratch_shapes=[
            row,
            row,
            pltpu.VMEM((blocks + pairs, BLK, BLK), bf16),
            pltpu.SemaphoreType.DMA((2,)),
            pltpu.SemaphoreType.DMA(((blocks + pairs) // 8,)),
        ],
        compiler_params=params(48),
        cost_estimate=pl.CostEstimate(
            flops=(blocks + pairs) * BLK * BLK * 100, bytes_accessed=1 << 20, transcendentals=0
        ),
        name="back_local",
    )(local_first, local_second, ratio, in_hbm(tiles))
    received2 = received2.reshape(places * 2, HALF)
    common = [sums, table, flat, pltpu.VMEM((held, BLK, BLK), bf16)]
    if keep:
        kernel, operands, specs = back_cross_kernel, (in_hbm(cross_tiles[0]),), [HBM]
        scratch = [pltpu.SemaphoreType.DMA((2,)), pltpu.SemaphoreType.DMA((places // 8,))]
    else:
        kernel, operands, specs = back_again_kernel, (received, near), [VMEM, VMEM]
        scratch = [square, square, pltpu.SemaphoreType.DMA((2,))]
    sensitivity = pl.pallas_call(
        functools.partial(kernel, 8 if keep else width),
        out_shape=shape((flat_rows, HALF), f32),
        in_specs=[SMEM, SMEM, HBM, VMEM, *specs, VMEM, HBM],
        out_specs=VMEM,
        scratch_shapes=common + scratch,
        compiler_params=params(48),
        name="back_cross",
    )(listed, size, chosen, received2, *operands, back, vol)
    return (filtered.reshape(-1), sensitivity.reshape(-1))


def solution(mesh):
    return jax.shard_map(
        shards,
        mesh=mesh,
        in_specs=(
            P(None, AXES),
            P(AXES),
            P(AXES),
            P(AXES),
            P(AXES),
            P(AXES),
            P(AXES, None),
            P(AXES, None, None),
        ),
        out_specs=(P(AXES), P(AXES)),
        check_vma=False,
    )
```

time: 342 us -> 60.4 us (0.18)
  the two profiles are of different devices: /device:TPU:0 before, /device:TPU:3 now
where the time goes in v1:
time: 60.4 us; the launch traced here: 59.9 us
  Pallas kernels  50.5 us (84%)
  starting transfers between devices  8.76 us (15%)
  between operations  0.69 us (1%)
    pallas_call x1, Pallas kernels, shards(): pl.pallas_call(functools.partial(local_kernel, width), out_shape=(shape((...  16.5 us
    pallas_call x1, Pallas kernels, shards(): pl.pallas_call(functools.partial(cross_kernel, width, keep), out_shape=(s...  15.6 us
    pallas_call x1, Pallas kernels, shards(): pl.pallas_call(functools.partial(back_local_kernel, 8), out_shape=shape((...  8.2 us
    pallas_call x1, Pallas kernels, shards(): pl.pallas_call(functools.partial(kernel, 8 if keep else width), out_shape...  8.03 us
    all_to_all x1, starting transfers between devices, shards(): lax.all_to_all(payload, AXES, split_axis=0, concat_axis=0, tiled=True)  6.45 us
    all_to_all x1, starting transfers between devices, shards(): lax.all_to_all(payload2, AXES, split_axis=0, concat_axis=0, tiled=True)  2.32 us
    pallas_call x1, Pallas kernels, shards(): pl.pallas_call(pack_kernel, out_shape=(shape((peers, PEER_ROWS, HALF), i3...  2.13 us
  transfers between devices with their start and end apart: 2, of which 0 were waited for; matrix products, arithmetic and copies ran while one was open for 0% of the time, Pallas kernels for 41%

profile of v1, /device:TPU:3, one launch (start us, length us, event | category | flops | bytes accessed | tf_op | source)
XLA Modules:
  0.0 59.9 jit_solution(14577228210920611532)
XLA Ops:
  0.6 2.1 %pack.1 = (s32[32,24,128]{2,1,0:T(8,128)}, s32[64,8,128]{2,1,0:T(8,128)S(1)}) custom-call(s32[4,32]{1,0:T(4,128)} %bitcast.17, f32[3,16384]{1,0:T(4,128)} %cent_in.1, f32[128,128]{1,0:T(8,128)} %bitcast.12, f32[128,128]{1,0:T(8,128)} %bitcast.16), custom_call_target="tpu_custom_call" | custom-call | tf_op jit(solution)/shard_map/pack/pallas_call | solution.py:502
  2.8 6.4 %all-to-all-start = ((s32[32,24,128]{2,1,0:T(8,128)}), s32[32,24,128]{2,1,0:T(8,128)S(1)}, u32[]{:S(2)}, u32[]{:S(2)}) async-start(s32[32,24,128]{2,1,0:T(8,128)} %get-tuple-element.16), calls=%async_computation | async-start | bytes 786432 | tf_op jit(solution)/shard_map/all_to_all | solution.py:517
  9.2 16.5 %local.1 = (f32[64,8,256]{2,1,0:T(8,128)S(1)}, bf16[128,256,256]{2,1,0:T(8,128)(2,1)}, bf16[64,32,256]{2,1,0:T(8,128)(2,1)S(1)}, s32[128]{0:T(128)S(1)}, s32[1]{0:T(128)}) custom-call(s32[64]{0:T(128)} %first_in.3, s32[64]{0:T(128)} %second_in.3, s32[1,32]{1,0:T(1,128)} %counts_in.1, s32[64,8,128]{2,1,0:T(8,128)S(1)} %get-tuple-element.13.words), custom_call_target="tpu_custom_call" | custom-call | flops 838860800 | bytes 1048576 | tf_op jit(solution)/shard_map/local/pallas_call | solution.py:518
  25.7 0.0 all-to-all-done
  25.8 15.6 %cross.1 = (f32[128,128]{1,0:T(8,128)}, f32[64,8,256]{2,1,0:T(8,128)S(1)}, f32[32,8,128]{2,1,0:T(8,128)}, bf16[128,256,256]{2,1,0:T(8,128)(2,1)}) custom-call(s32[128]{0:T(128)S(1)} %get-tuple-element.14.listed, s32[1]{0:T(128)} %get-tuple-element.15.size, s32[4,32]{1,0:T(4,128)} %bitcast.18, s32[768,128]{1,0:T(8,128)S(1)} %bitcast.10, ...), custom_call_target="tpu_custom_call" | custom-call | tf_op jit(solution)/shard_map/cross/pallas_call | solution.py:552
  41.3 2.3 %all-to-all-start.1 = ((f32[32,8,128]{2,1,0:T(8,128)}), f32[32,8,128]{2,1,0:T(8,128)S(1)}, u32[]{:S(2)}, u32[]{:S(2)}) async-start(f32[32,8,128]{2,1,0:T(8,128)} %get-tuple-element.20), calls=%async_computation.1 | async-start | bytes 262144 | tf_op jit(solution)/shard_map/all_to_all | solution.py:577
  43.7 8.2 %back_local.1.total_in = f32[64,8,256]{2,1,0:T(8,128)S(1)} custom-call(s32[64]{0:T(128)} %first_in.3, s32[64]{0:T(128)} %second_in.3, f32[64,8,256]{2,1,0:T(8,128)S(1)} %get-tuple-element.22.ratio, bf16[128,256,256]{2,1,0:T(8,128)(2,1)} %get-tuple-element.23.kept), custom_call_target="tpu_custom_call" | custom-call | flops 838860800 | bytes 1048576 | tf_op jit(solution)/shard_map/back_local/pallas_call | solution.py:578
  51.9 0.0 all-to-all-done.1
  51.9 8.0 %back_cross.1 = f32[128,128]{1,0:T(8,128)} custom-call(s32[128]{0:T(128)S(1)} %get-tuple-element.14.listed, s32[1]{0:T(128)} %get-tuple-element.15.size, s32[4,32]{1,0:T(4,128)} %bitcast.19, f32[256,128]{1,0:T(8,128)S(1)} %bitcast.11, bf16[128,256,256]{2,1,0:T(8,128)(2,1)} %get-tuple-element.21.kept, f32[64,8,256]{2,1,0:T(8,128)S(1)} %back_local.1.total_in, ...), custom_call_target="tpu_custom_call" | custom-call | tf_op jit(solution)/shard_map/back_cross/pallas_call | solution.py:604
Async XLA Ops:
  2.8 23.0 %all-to-all-start = ((s32[32,24,128]{2,1,0:T(8,128)}), s32[32,24,128]{2,1,0:T(8,128)S(1)}, u32[]{:S(2)}, u32[]{:S(2)}) async-start(s32[32,24,128]{2,1,0:T(8,128)} %get-tuple-element.16), calls=%async_computation | async-start | bytes 786432 | tf_op jit(solution)/shard_map/all_to_all | solution.py:517
  41.3 10.5 %all-to-all-start.1 = ((f32[32,8,128]{2,1,0:T(8,128)}), f32[32,8,128]{2,1,0:T(8,128)S(1)}, u32[]{:S(2)}, u32[]{:S(2)}) async-start(f32[32,8,128]{2,1,0:T(8,128)} %get-tuple-element.20), calls=%async_computation.1 | async-start | bytes 262144 | tf_op jit(solution)/shard_map/all_to_all | solution.py:577
